TPU v7x, 256 devices: a whole 4x4x8 slice. The times are simulated.
256 devices in a mesh: row: 64 (over z, y, x_hi), col: 2 (over core), layer: 2 (over x_lo).
Axes of the slice: x: 4 (x_hi: 2, x_lo: 2; x = x_hi * 2 + x_lo), y: 4, z: 8, core: 2. Of those that a mesh axis runs over, the one named last changes fastest.
Arguments:
- a_blocks: bfloat16 [64, 128, 64, 64], P('row', ('col', 'layer')), may hold values from -6 to 6
- a_index: int32 [64, 128, 2], P('row', ('col', 'layer')), may hold values from 0 to 511, as said below
- a_count: int32 [64, 4], P('row', ('col', 'layer')), may hold values from 1 to 32, as said below
- b_blocks: bfloat16 [512, 2, 64, 64], P(('row', 'layer'), 'col'), may hold values from -0.75 to 0.75
- b_index: int32 [512, 2, 2], P(('row', 'layer'), 'col'), may hold values from 0 to 15, as said below
- b_count: int32 [128, 2], P(('row', 'layer'), 'col'), may hold values from 1 to 4, as said below
Outputs:
- product: bfloat16 [32768, 1024], P(('row', 'layer'), 'col')
Inputs may be any that keep to these rules, and one draw needn't show every extreme that they name: `a_index`: within one piece the live slots name distinct (block row, inner block) positions; entry 0 is below 8, entry 1 below 512. `b_index`: within one piece the live slots name distinct (inner block, block column) positions; entry 0 is below 16, entry 1 below 8. `a_count`: some piece is full. `b_count`: some piece is full.
All inputs are finite; a program needn't handle non-finite values.
Results may differ from a plain program's by a relative error of at most 0.001.
Values may be sent and summed in bfloat16 or wider, within the bound.
No kernel may reach another device: no remote copies, remote signals or barrier semaphores. Data moves between devices by JAX's collectives and lax.ppermute only.
A program may use at most 128 MiB of HBM per device.

v0:
```python
import math
import jax
import jax.numpy as jnp
from jax import lax
from jax.sharding import PartitionSpec as P

BLK = 64
NB = 2048
RW = 8
KW = 8


def tile_product(a_vals, a_rows, a_keys, b_vals, b_keys, b_cols, row_count, col_count):
    count = b_vals.shape[0]
    hit = (a_keys[:, None, None] == b_keys[None, None, :]) & (
        b_cols[None, None, :] == jnp.arange(col_count, dtype=jnp.int32)[None, :, None]
    )
    chosen = jnp.sum(jnp.where(hit, jnp.arange(count, dtype=jnp.int32)[None, None, :], 0), axis=2)
    found = jnp.any(hit, axis=2)
    picked = b_vals[chosen] * found[:, :, None, None].astype(b_vals.dtype)
    terms = jnp.einsum("axy,ajyz->axjz", a_vals, picked, preferred_element_type=jnp.float32)
    place = (a_rows[:, None] == jnp.arange(row_count, dtype=jnp.int32)[None, :]).astype(jnp.float32)
    summed = jnp.dot(place.T, terms.reshape(terms.shape[0], -1), precision=lax.Precision.HIGHEST)
    return summed.reshape(row_count * BLK, col_count * BLK)


def on_device(a_blocks, a_index, a_count, b_blocks, b_index, b_count):
    slots_a = a_blocks.shape[1]
    slots_b = b_blocks.shape[0]
    layers = lax.axis_size("layer")
    inner_a = NB // (layers * lax.axis_size("col"))
    inner_b = NB // (layers * lax.axis_size("row"))
    a_keys = jnp.where(jnp.arange(slots_a, dtype=jnp.int32) < a_count[0, 0], a_index[0, :, 1], -1)[
        None, :
    ]
    a_rows = a_index[0, :, 0][None, :]
    b_keys = jnp.where(jnp.arange(slots_b, dtype=jnp.int32) < b_count[0, 0], b_index[:, 0, 0], -1)[
        :, None
    ]
    b_cols = b_index[:, 0, 1][:, None]
    b_vals, b_raw, b_col_all = (
        lax.all_gather(b_blocks, "row", axis=0, tiled=True),
        lax.all_gather(b_keys, "row", axis=0, tiled=True),
        lax.all_gather(b_cols, "row", axis=0, tiled=True),
    )
    piece_b = jnp.arange(b_raw.shape[0], dtype=jnp.int32) // slots_b
    b_glob = jnp.where(b_raw[:, 0] >= 0, piece_b * inner_b + b_raw[:, 0], -2).astype(jnp.int32)
    row_count = RW
    b_flat = b_vals[:, 0]
    b_col_flat = b_col_all[:, 0]
    empty = jnp.zeros((row_count * BLK, KW * BLK), jnp.float32)

    def fold_rows(total, vals, rows, glob):
        taken = glob.shape[0]
        step = slots_a * math.gcd(taken // slots_a, 8)
        turns = taken // step

        def one_turn(index, acc):
            return acc + tile_product(vals, rows, glob, b_flat, b_glob, b_col_flat, row_count, KW)

        return lax.fori_loop(0, turns, one_turn, total)

    vals = lax.all_gather(a_blocks, "col", axis=1, tiled=True)
    keys = lax.all_gather(a_keys, "col", axis=1, tiled=True)
    rows = lax.all_gather(a_rows, "col", axis=1, tiled=True)
    taken = keys.shape[1]
    group = jnp.arange(taken, dtype=jnp.int32) // slots_a
    glob = jnp.where(keys[0] >= 0, group * inner_a + keys[0], -1).astype(jnp.int32)
    partial_tile = fold_rows(empty, vals[0], rows[0], glob)
    return lax.psum_scatter(partial_tile, "layer", scatter_dimension=0, tiled=True).astype(
        jnp.bfloat16
    )


def solution(mesh):
    in_specs = (
        P("row", ("col", "layer"), None, None),
        P("row", ("col", "layer"), None),
        P("row", ("col", "layer")),
        P(("row", "layer"), "col", None, None),
        P(("row", "layer"), "col", None),
        P(("row", "layer"), "col"),
    )
    out_specs = P(("row", "layer"), "col")
    return jax.shard_map(
        on_device, mesh=mesh, in_specs=in_specs, out_specs=out_specs, check_vma=False
    )
```

profile of v0, /device:TPU:1, one launch (start us, length us, event | category | flops | bytes accessed | tf_op | source)
XLA Modules:
  0.0 255.7 jit_solution(8151125068441532517)
XLA Ops:
  6.5 0.7 all-gather.4.cloned.1.call-update
  8.6 1.3 dynamic-slice.2
  9.9 1.3 dynamic-slice
  12.4 0.8 bitcast_dynamic-update-slice_fusion.1
  13.2 0.8 fusion.11
  14.0 4.7 %all-reduce.5 = (s32[64]{0:T(128)S(1)}, s32[64]{0:T(128)S(1)}) all-reduce(s32[64]{0:T(128)S(1)} %fusion.11, s32[64]{0:T(128)S(1)} %bitcast_dynamic-update-slice_fusion.1), channel_id=1, replica_groups=mesh['row'=64,'col'=2,'layer'=2] {'col'}, use_global_device_ids=true, to_apply=%add.1 | all-reduce | flops 128 | bytes 1024 | tf_op jit(solution)/shard_map/squeeze | solution.py:68
  18.7 0.8 bitcast_dynamic-update-slice_fusion
  19.5 0.8 fusion.13
  20.2 21.5 %all-reduce.4 = (s32[256]{0:T(256)S(1)}, s32[256]{0:T(256)S(1)}) all-reduce(s32[256]{0:T(256)S(1)} %bitcast_dynamic-update-slice_fusion, s32[256]{0:T(256)S(1)} %fusion.13), channel_id=3, replica_groups=mesh['row'=64,'col'=2,'layer'=2] {'row'}, use_global_device_ids=true, to_apply=%add.3 | all-reduce | flops 512 | bytes 4096
  41.7 0.1 broadcast_compare_fusion
  41.8 1.2 and_reduce_fusion
  43.0 1.2 fusion.3
  44.2 0.1 reshape.170
  44.3 7.5 %all_gather.23 = bf16[1,64,64,64]{3,2,0,1:T(8,128)(2,1)S(1)} all-gather(bf16[1,32,64,64]{3,2,0,1:T(8,128)(2,1)} %bitcast.42), channel_id=1, replica_groups=mesh['row'=64,'col'=2,'layer'=2] {'col'}, dimensions={1}, use_global_device_ids=true | all-gather | bytes 786432 | tf_op jit(solution)/shard_map/all_gather | solution.py:63
  51.8 87.9 %all-gather.4.cloned.1.call-done = bf16[256,1,64,64]{3,2,1,0:T(8,128)(2,1)} async-done(((bf16[4,1,64,64]{3,2,1,0:T(8,128)(2,1)}), bf16[256,1,64,64]{3,2,1,0:T(8,128)(2,1)}) %all-gather.4.cloned.1.call-update) | async-done | bytes 2097168 | tf_op jit(solution)/shard_map/all_gather | solution.py:42
  139.6 21.7 %gather_fusion = bf16[512,64,64]{2,1,0:T(8,128)(2,1)} fusion(bf16[256,64,64]{2,1,0:T(8,128)(2,1)} %bitcast.41, s32[1024]{0:T(1024)S(1)} %pad_clamp_fusion), kind=kCustom, calls=%fused_computation | custom fusion | bytes 8390656 | tf_op jit(solution)/shard_map/while/body/eval_jaxpr/gather | solution.py:20
  161.4 11.9 %copy.13 = bf16[64,8,64,64]{2,3,1,0:T(8,128)(2,1)} copy(bf16[64,8,64,64]{3,2,1,0:T(8,128)(2,1)} %bitcast.40) | data formatting | bytes 8388608 | tf_op jit(solution)/shard_map/while/body/eval_jaxpr/gather | solution.py:20
  173.3 11.5 %convolution_bitcast_fusion = f32[64,64,8,64]{1,3,2,0:T(8,128)} fusion(bf16[64,8,64,64]{2,3,1,0:T(8,128)(2,1)} %copy.13, bf16[64,8]{1,0:T(8,128)(2,1)S(1)} %convert_element_type.14, bf16[1,64,64,64]{3,2,0,1:T(8,128)(2,1)S(1)} %all_gather.23), kind=kOutput, calls=%fused_computation.1 | convolution fusion | flops 270532608 | bytes 13108224 | tf_op jit(solution)/shard_map/while/body/eval_jaxpr/axy,ajyz->axjz/dot_general | solution.py:21
  184.8 17.5 %copy.15 = f32[64,64,8,64]{3,2,1,0:T(8,128)} copy(f32[64,64,8,64]{1,3,2,0:T(8,128)} %convolution_bitcast_fusion) | data formatting | bytes 16777216 | tf_op jit(solution)/shard_map/while/body/eval_jaxpr/axy,ajyz->axjz/dot_general | solution.py:21
  202.2 12.9 %reshape.166 = f32[64,32768]{1,0:T(8,128)} reshape(f32[64,64,8,64]{3,2,1,0:T(8,128)} %copy.15) | data formatting | bytes 16777216 | tf_op jit(solution)/shard_map/while/body/eval_jaxpr/reshape | solution.py:23
  215.1 5.2 %fusion.4 = f32[8,32768]{1,0:T(8,128)S(1)} fusion(f32[64,32768]{1,0:T(8,128)} %reshape.166, s32[64]{0:T(128)S(1)} %get-tuple-element.22), kind=kOutput, calls=%fused_computation.11 | convolution fusion | flops 201327104 | bytes 9437440 | tf_op jit(solution)/shard_map/while/body/eval_jaxpr/dot_general | solution.py:23
  220.3 1.2 reshape.167
  221.5 25.6 %reduce-scatter.2.cloned.1.call-done = f32[256,512]{1,0:T(8,128)} async-done(((f32[512,512]{1,0:T(8,128)}), f32[256,512]{1,0:T(8,128)}) %reduce-scatter.2.cloned.1.call-update) | async-done | bytes 524304 | tf_op jit(solution)/shard_map/reduce_scatter | solution.py:70
  247.1 1.8 convert_element_type.15
  (13 shorter events, 0.1 us)
Async XLA Ops:
  6.5 133.1 %all-gather.4.cloned.1.call-start = ((), (), s32[]{:S(2)}) async-start(), calls=%async_computation.1 | async-start | bytes 4259840 | tf_op jit(solution)/shard_map/all_gather | solution.py:42
  7.3 239.8 %reduce-scatter.2.cloned.1.call-start = ((), (), s32[]{:S(2)}) async-start(), calls=%async_computation.2 | async-start | bytes 1572864 | tf_op jit(solution)/shard_map/reduce_scatter | solution.py:70
Sparse Core Ops, SparseCore 0:
  11.1 128.4 all-gather.3
  221.6 25.4 reduce-scatter.1
where the time goes:
time: 257 us; the launch traced here: 256 us
  waiting for transfers between devices  114 us (44%)
  local copies, waits for them, and re-layouts  69.4 us (27%)
  blocking collectives  33.6 us (13%)
  matrix products  16.7 us (6%)
  between operations  16 us (6%)
  other arithmetic  5.76 us (2%)
    all_gather x1, waiting for transfers between devices, on_device(): lax.all_gather(b_blocks, 'row', axis=0, tiled=True)  87.9 us
    gather x2, local copies, waits for them, and re-layouts, tile_product(): picked = b_vals[chosen] * found[:, :, None, None].astype(b_vals.dtype)  33.7 us
    reduce_scatter x1, waiting for transfers between devices, on_device(): lax.psum_scatter(partial_tile, 'layer', scatter_dimension=0, tiled=True)  25.6 us
    unnamed x1, blocking collectives  21.5 us
    dot_general x1, local copies, waits for them, and re-layouts, tile_product(): jnp.einsum('axy,ajyz->axjz', a_vals, picked, preferred_element_type=jnp.f...  17.5 us
    reshape x1, local copies, waits for them, and re-layouts, tile_product(): terms.reshape(terms.shape[0], -1)  12.9 us
    dot_general x1, matrix products, tile_product(): jnp.einsum('axy,ajyz->axjz', a_vals, picked, preferred_element_type=jnp.f...  11.5 us
    all_gather x1, blocking collectives, on_device(): vals = lax.all_gather(a_blocks, 'col', axis=1, tiled=True)  7.45 us
  transfers between devices with their start and end apart: 2, of which 2 were waited for; matrix products, arithmetic and copies ran while one was open for 3% of the time, Pallas kernels for 0%

commit v1 on v0

--- a/solution.py
+++ b/solution.py
@@ -39,7 +39,15 @@
     ]
     b_cols = b_index[:, 0, 1][:, None]
     b_vals, b_raw, b_col_all = (
-        lax.all_gather(b_blocks, "row", axis=0, tiled=True),
+        jnp.concatenate(
+            lax.all_to_all(
+                jnp.stack(lax.psum(1, "row") * [b_blocks], axis=0),
+                "row",
+                split_axis=0,
+                concat_axis=0,
+            ),
+            axis=0,
+        ),
         lax.all_gather(b_keys, "row", axis=0, tiled=True),
         lax.all_gather(b_cols, "row", axis=0, tiled=True),
     )

time: 257 us -> 214 us (0.83)
  waiting for transfers between devices: 114 us -> 24.8 us
  blocking collectives: 33.6 us -> 53.4 us
  starting transfers between devices: 0.04 us -> 15.2 us
  local copies, waits for them, and re-layouts: 69.4 us -> 82.2 us
    all_gather x1 -> x0, waiting for transfers between devices: 87.9 us -> none  [on_device(): lax.all_gather(b_blocks, 'row', axis=0, tiled=True)]
    unnamed x1, blocking collectives: 21.5 us -> 46.5 us
    all_to_all x0 -> x1, starting transfers between devices: none -> 15.1 us  [on_device(): lax.all_to_all(jnp.stack(lax.psum(1, 'row') * [b_blocks], axis=0), 'row',...]
    unnamed x8 -> x23, local copies, waits for them, and re-layouts: 4.1 us -> 17.1 us
    all_gather x1, blocking collectives: 7.45 us -> 4.44 us  [on_device(): vals = lax.all_gather(a_blocks, 'col', axis=1, tiled=True)]
  transfers between devices with their start and end apart: 2 -> 2, of which waited for: 2 -> 1; matrix products, arithmetic and copies ran while one was open for 3% -> 2% of each run, Pallas kernels for 0% -> 0%
where the time goes in v1:
time: 214 us; the launch traced here: 213 us
  local copies, waits for them, and re-layouts  82.2 us (38%)
  blocking collectives  53.4 us (25%)
  waiting for transfers between devices  24.8 us (12%)
  matrix products  16.7 us (8%)
  between operations  16.1 us (8%)
  starting transfers between devices  15.2 us (7%)
  other arithmetic  4.41 us (2%)
    unnamed x1, blocking collectives  46.5 us
    gather x2, local copies, waits for them, and re-layouts, tile_product(): picked = b_vals[chosen] * found[:, :, None, None].astype(b_vals.dtype)  33.5 us
    reduce_scatter x1, waiting for transfers between devices, on_device(): lax.psum_scatter(partial_tile, 'layer', scatter_dimension=0, tiled=True)  24.8 us
    dot_general x1, local copies, waits for them, and re-layouts, tile_product(): jnp.einsum('axy,ajyz->axjz', a_vals, picked, preferred_element_type=jnp.f...  17.5 us
    unnamed x23, local copies, waits for them, and re-layouts  17.1 us
    all_to_all x1, starting transfers between devices, on_device(): lax.all_to_all(jnp.stack(lax.psum(1, 'row') * [b_blocks], axis=0), 'row',...  15.1 us
    reshape x1, local copies, waits for them, and re-layouts, tile_product(): terms.reshape(terms.shape[0], -1)  12.9 us
    dot_general x1, matrix products, tile_product(): jnp.einsum('axy,ajyz->axjz', a_vals, picked, preferred_element_type=jnp.f...  11.5 us
  transfers between devices with their start and end apart: 2, of which 1 were waited for; matrix products, arithmetic and copies ran while one was open for 2% of the time, Pallas kernels for 0%

profile of v1, /device:TPU:1, one launch (start us, length us, event | category | flops | bytes accessed | tf_op | source)
XLA Modules:
  0.0 212.8 jit_solution(14727403905578967136)
XLA Ops:
  6.5 0.8 copy-done
  7.4 3.0 %broadcast_bitcast_fusion = bf16[64,1,4,64,64]{4,3,2,1,0:T(8,128)(2,1)} fusion(bf16[4,64,64]{2,1,0:T(8,128)(2,1)S(1)} %bitcast.44), kind=kLoop, calls=%fused_computation.37 | loop fusion | bytes 2129920
  10.4 7.9 %reshape.209 = bf16[64,2,8192]{2,1,0:T(2,128)(2,1)} reshape(bf16[64,1,4,64,64]{4,3,2,1,0:T(8,128)(2,1)} %broadcast_bitcast_fusion) | data formatting | bytes 4194304
  18.2 15.1 %all-to-all-start = ((bf16[64,2,8192]{2,1,0:T(2,128)(2,1)}), bf16[64,2,8192]{2,1,0:T(2,128)(2,1)S(1)}, u32[]{:S(2)}, u32[]{:S(2)}) async-start(bf16[64,2,8192]{2,1,0:T(2,128)(2,1)} %reshape.209), calls=%async_computation | async-start | bytes 4194304 | tf_op jit(solution)/shard_map/all_to_all | solution.py:43
  34.7 0.6 dynamic-slice.2
  35.3 0.6 dynamic-slice
  37.2 0.1 bitcast_dynamic-update-slice_fusion.1
  37.3 0.1 fusion.11
  37.4 2.4 %all-reduce.5 = (s32[64]{0:T(128)S(1)}, s32[64]{0:T(128)S(1)}) all-reduce(s32[64]{0:T(128)S(1)} %fusion.11, s32[64]{0:T(128)S(1)} %bitcast_dynamic-update-slice_fusion.1), channel_id=1, replica_groups=mesh['row'=64,'col'=2,'layer'=2] {'col'}, use_global_device_ids=true, to_apply=%add.1 | all-reduce | flops 128 | bytes 1024 | tf_op jit(solution)/shard_map/squeeze | solution.py:76
  39.9 0.1 fusion.13
  40.0 46.5 %all-reduce.4 = (s32[256]{0:T(256)S(1)}, s32[256]{0:T(256)S(1)}) all-reduce(s32[256]{0:T(256)S(1)} %bitcast_dynamic-update-slice_fusion, s32[256]{0:T(256)S(1)} %fusion.13), channel_id=3, replica_groups=mesh['row'=64,'col'=2,'layer'=2] {'row'}, use_global_device_ids=true, to_apply=%add.3 | all-reduce | flops 512 | bytes 4096
  86.7 1.2 and_reduce_fusion
  87.9 1.2 fusion.3
  89.2 4.4 %all_gather.19 = bf16[1,64,64,64]{3,2,0,1:T(8,128)(2,1)S(1)} all-gather(bf16[1,32,64,64]{3,2,0,1:T(8,128)(2,1)} %bitcast.47), channel_id=1, replica_groups=mesh['row'=64,'col'=2,'layer'=2] {'col'}, dimensions={1}, use_global_device_ids=true | all-gather | bytes 786432 | tf_op jit(solution)/shard_map/all_gather | solution.py:71
  93.6 4.0 %reshape.210 = bf16[64,1,4,64,64]{4,3,2,1,0:T(8,128)(2,1)} reshape(bf16[64,2,8192]{2,1,0:T(2,128)(2,1)S(1)} %all-to-all-done) | data formatting | bytes 4194304
  97.6 21.6 %gather_fusion = bf16[512,64,64]{2,1,0:T(8,128)(2,1)} fusion(bf16[256,64,64]{2,1,0:T(8,128)(2,1)} %bitcast.45, s32[1024]{0:T(1024)S(1)} %pad_clamp_fusion), kind=kCustom, calls=%fused_computation | custom fusion | bytes 8390656 | tf_op jit(solution)/shard_map/while/body/eval_jaxpr/gather | solution.py:20
  119.2 11.9 %copy.12 = bf16[64,8,64,64]{2,3,1,0:T(8,128)(2,1)} copy(bf16[64,8,64,64]{3,2,1,0:T(8,128)(2,1)} %bitcast.46) | data formatting | bytes 8388608 | tf_op jit(solution)/shard_map/while/body/eval_jaxpr/gather | solution.py:20
  131.1 11.5 %convolution_bitcast_fusion = f32[64,64,8,64]{1,3,2,0:T(8,128)} fusion(bf16[64,8,64,64]{2,3,1,0:T(8,128)(2,1)} %copy.12, bf16[64,8]{1,0:T(8,128)(2,1)S(1)} %convert_element_type.14, bf16[1,64,64,64]{3,2,0,1:T(8,128)(2,1)S(1)} %all_gather.19), kind=kOutput, calls=%fused_computation.1 | convolution fusion | flops 270532608 | bytes 13108224 | tf_op jit(solution)/shard_map/while/body/eval_jaxpr/axy,ajyz->axjz/dot_general | solution.py:21
  142.6 17.5 %copy.14 = f32[64,64,8,64]{3,2,1,0:T(8,128)} copy(f32[64,64,8,64]{1,3,2,0:T(8,128)} %convolution_bitcast_fusion) | data formatting | bytes 16777216 | tf_op jit(solution)/shard_map/while/body/eval_jaxpr/axy,ajyz->axjz/dot_general | solution.py:21
  160.1 12.9 %reshape.169 = f32[64,32768]{1,0:T(8,128)} reshape(f32[64,64,8,64]{3,2,1,0:T(8,128)} %copy.14) | data formatting | bytes 16777216 | tf_op jit(solution)/shard_map/while/body/eval_jaxpr/reshape | solution.py:23
  173.0 5.2 %fusion.4 = f32[8,32768]{1,0:T(8,128)S(1)} fusion(f32[64,32768]{1,0:T(8,128)} %reshape.169, s32[64]{0:T(128)S(1)} %get-tuple-element.22), kind=kOutput, calls=%fused_computation.11 | convolution fusion | flops 201327104 | bytes 9437440 | tf_op jit(solution)/shard_map/while/body/eval_jaxpr/dot_general | solution.py:23
  178.2 1.2 reshape.170
  179.4 24.8 %reduce-scatter.2.cloned.1.call-done = f32[256,512]{1,0:T(8,128)} async-done(((f32[512,512]{1,0:T(8,128)}), f32[256,512]{1,0:T(8,128)}) %reduce-scatter.2.cloned.1.call-update) | async-done | bytes 524304 | tf_op jit(solution)/shard_map/reduce_scatter | solution.py:78
  204.2 1.8 convert_element_type.15
  (27 shorter events, 0.4 us)
Async XLA Ops:
  6.5 0.8 copy-start
  6.5 28.2 %copy-start.5 = (u32[256]{0:T(256)S(1)}, u32[256]{0:T(256)}, u32[]{:S(2)}) copy-start(u32[256]{0:T(256)} %constant.74) | copy-start | bytes 3076
  6.5 28.8 %copy-start.4 = (u32[256]{0:T(256)S(1)}, u32[256]{0:T(256)}, u32[]{:S(2)}) copy-start(u32[256]{0:T(256)} %constant.64) | copy-start | bytes 3076
  6.5 30.7 %copy-start.2 = (s32[1,32,2]{1,2,0:T(2,128)S(1)}, s32[1,32,2]{1,2,0:T(2,128)}, u32[]{:S(2)}) copy-start(s32[1,32,2]{1,2,0:T(2,128)} %param.7) | copy-start | bytes 772
  6.5 33.3 %copy-start.3 = (s32[4,1,2]{0,2,1:T(2,128)S(1)}, s32[4,1,2]{0,2,1:T(2,128)}, u32[]{:S(2)}) copy-start(s32[4,1,2]{0,2,1:T(2,128)} %param.10) | copy-start | bytes 100
  18.2 75.4 %all-to-all-start = ((bf16[64,2,8192]{2,1,0:T(2,128)(2,1)}), bf16[64,2,8192]{2,1,0:T(2,128)(2,1)S(1)}, u32[]{:S(2)}, u32[]{:S(2)}) async-start(bf16[64,2,8192]{2,1,0:T(2,128)(2,1)} %reshape.209), calls=%async_computation | async-start | bytes 4194304 | tf_op jit(solution)/shard_map/all_to_all | solution.py:43
  33.4 170.8 %reduce-scatter.2.cloned.1.call-start = ((), (), s32[]{:S(2)}) async-start(), calls=%async_computation.2 | async-start | bytes 1572864 | tf_op jit(solution)/shard_map/reduce_scatter | solution.py:78
  160.1 45.9 %copy-start.1 = (bf16[4,1,64,64]{3,2,1,0:T(8,128)(2,1)S(1)}, bf16[4,1,64,64]{3,2,1,0:T(8,128)(2,1)}, u32[]{:S(2)}) copy-start(bf16[4,1,64,64]{3,2,1,0:T(8,128)(2,1)} %param.9) | copy-start | bytes 98308
Sparse Core Ops, SparseCore 0:
  179.5 24.6 reduce-scatter.1
